TPU v7x, 256 devices: a whole 4x4x8 slice. The times are simulated.
256 devices in a mesh: ctx: 32 (over x, z), cls: 8 (over y, core).
Axes of the slice: x: 4, y: 4, z: 8, core: 2. Of those that a mesh axis runs over, the one named last changes fastest.
Arguments:
- tokens: bfloat16 [196608, 8192], P(('ctx', 'cls')), may hold values from -80 to 80
- doc_length: int32 [1], replicated, may hold values from 98304 to 196608
- queries: bfloat16 [64, 8192], P('cls', 'ctx'), may hold values from -0.046875 to 0.046875
- norm_gain: float32 [8192], P('ctx'), may hold values from 0.1 to 1.9
- head_weight: bfloat16 [8192, 4096], P('ctx', 'cls'), may hold values from -0.0625 to 0.0625
- head_bias: float32 [4096], P('cls'), may hold values from -20 to 20
- labels: int32 [4096], P('cls'), may hold values 0 or 1
Outputs:
- mean_loss: float32 [], replicated
- query_grad: float32 [64, 8192], P('cls', 'ctx')
- head_grad: float32 [8192, 4096], P('ctx', 'cls')
- bias_grad: float32 [4096], P('cls')
All inputs are finite; a program needn't handle non-finite values. No bound on the sum of `labels` on one device may be relied on, other than what follows from the above.
Results may differ from a plain program's by a relative error of at most 0.017.
Values may be sent and summed in bfloat16 or wider, within the bound.
A program may use at most 64 MiB of HBM per device.

v0:
```python
import jax
import jax.numpy as jnp
from jax import lax
from jax.sharding import PartitionSpec as P


def shards(tokens, doc_length, queries, norm_gain, head_weight, head_bias, labels):
    context_count = lax.axis_size("ctx")
    class_count = lax.axis_size("cls")
    context_index = lax.axis_index("ctx")
    class_index = lax.axis_index("cls")
    token_count = tokens.shape[0]
    query_share = queries.shape[0]
    width_share = queries.shape[1]
    full_width = width_share * context_count

    def project_add(block_piece):
        return lax.dot_general(
            block_piece, tokens, (((1,), (1,)), ((), ())), preferred_element_type=jnp.float32
        )

    query_block = lax.all_gather(queries, "cls", axis=0, tiled=True)
    scores = project_add(lax.all_gather(query_block, "ctx", axis=1, tiled=True))
    offset = (context_index * class_count + class_index) * token_count
    position = offset + jnp.arange(token_count, dtype=jnp.int32)
    valid_mask = (position < doc_length[0])[None, :]
    local_peak = jnp.max(jnp.where(valid_mask, scores, -1e30), axis=1)
    peak = lax.pmax(local_peak, ("ctx", "cls"))
    weights = jnp.exp(jnp.where(valid_mask, scores - peak[:, None], -1e30))
    pooled_part = jnp.dot(weights.astype(jnp.bfloat16), tokens, preferred_element_type=jnp.float32)
    whole_sum = lax.psum(pooled_part, ("ctx", "cls"))
    pooled = lax.dynamic_slice(
        whole_sum,
        (class_index * query_share, context_index * width_share),
        (query_share, width_share),
    )
    scaled_b = (pooled * norm_gain[None, :]).astype(jnp.bfloat16)
    head_blocks = head_weight.reshape(width_share, query_share, -1)
    square_part = jnp.sum(pooled * pooled, axis=1)
    logit_part = jnp.einsum("hd,dha->ha", scaled_b, head_blocks, preferred_element_type=jnp.float32)
    squares, logit_raw = lax.psum((square_part, logit_part), "ctx")
    inverse_rms = lax.rsqrt(squares / full_width + 1e-05)
    logits = inverse_rms[:, None] * logit_raw + head_bias.reshape(query_share, -1)
    target = labels.reshape(query_share, -1).astype(jnp.float32)
    loss_part = jnp.sum(jax.nn.softplus(logits) - target * logits)
    mean_loss = lax.psum(loss_part, "cls") / (labels.shape[0] * class_count)
    logit_grad = jax.nn.sigmoid(logits) - target
    normed = pooled * inverse_rms[:, None] * norm_gain[None, :]
    head_grad = jnp.einsum("hd,ha->dha", normed, logit_grad).reshape(width_share, -1)
    normed_grad = (
        jnp.einsum("dha,ha->hd", head_blocks.astype(jnp.float32), logit_grad) * norm_gain[None, :]
    )
    unit_pooled = pooled * inverse_rms[:, None]
    inner_part = jnp.sum(unit_pooled * normed_grad, axis=1)
    inner_mean = lax.psum(inner_part, "ctx") / full_width
    pooled_grad = (inverse_rms[:, None] * (normed_grad - unit_pooled * inner_mean[:, None])).astype(
        jnp.bfloat16
    )
    grad_block = lax.all_gather(pooled_grad, "cls", axis=0, tiled=True)
    projected = project_add(lax.all_gather(grad_block, "ctx", axis=1, tiled=True))
    score_grad = (weights * projected).astype(jnp.bfloat16)
    query_part = jnp.dot(score_grad, tokens, preferred_element_type=jnp.float32)
    column_grad = lax.psum_scatter(query_part, "ctx", scatter_dimension=1, tiled=True)
    query_grad = lax.psum_scatter(column_grad, "cls", scatter_dimension=0, tiled=True)
    return (mean_loss, query_grad, head_grad, logit_grad.reshape(-1))


def solution(mesh):
    return jax.shard_map(
        shards,
        mesh=mesh,
        in_specs=(
            P(("ctx", "cls"), None),
            P(),
            P("cls", "ctx"),
            P("ctx"),
            P("ctx", "cls"),
            P("cls"),
            P("cls"),
        ),
        out_specs=(P(), P("cls", "ctx"), P("ctx", "cls"), P("cls")),
        check_vma=False,
    )
```

profile of v0, /device:TPU:1, one launch (start us, length us, event | category | flops | bytes accessed | tf_op | source)
XLA Modules:
  0.0 942.2 jit_solution(2797138843445842792)
XLA Ops:
  7.2 0.0 all-gather.3.cloned.1.call-start
  7.2 16.9 %all_gather.12 = bf16[64,256]{1,0:T(8,128)(2,1)} all-gather(bf16[8,256]{1,0:T(8,128)(2,1)} %param.9), channel_id=1, replica_groups=mesh['ctx'=32,'cls'=8] {'cls'}, dimensions={0}, use_global_device_ids=true | all-gather | bytes 36864 | tf_op jit(solution)/shard_map/all_gather | solution.py:22
  24.1 0.0 all-gather.3.cloned.1.call-update
  24.1 0.0 all-reduce.3.cloned.1.call-start
  24.8 67.0 %all-gather.3.cloned.1.call-done = bf16[64,8192]{1,0:T(8,128)(2,1)} async-done(((bf16[64,256]{1,0:T(8,128)(2,1)}), bf16[64,8192]{1,0:T(8,128)(2,1)}) %all-gather.3.cloned.1.call-update) | async-done | bytes 1048592 | tf_op jit(solution)/shard_map/all_gather | solution.py:23
  91.8 8.9 select_reduce_fusion
  100.8 79.1 %pmax.7 = f32[64]{0:T(128)S(1)} all-reduce(f32[64]{0:T(128)S(1)} %get-tuple-element.16), channel_id=1, replica_groups=mesh['ctx'=32,'cls'=8] {'ctx','cls'}, use_global_device_ids=true, to_apply=%region_1.2 | all-reduce | flops 64 | bytes 512 | tf_op jit(solution)/shard_map/pmax | solution.py:28
  180.0 8.2 fusion.3
  188.2 0.0 all-gather.5.cloned.1.call-start
  188.3 0.1 copy.12
  188.5 0.1 convert_element_type.22
  188.6 0.1 reshape.32
  188.6 255.2 %all-reduce.3.cloned.1.call-done = f32[64,8192]{1,0:T(8,128)} async-done(((f32[64,8192]{1,0:T(8,128)}), f32[64,8192]{1,0:T(8,128)}) %all-reduce.3.cloned.1.call-update) | async-done | bytes 2097168 | tf_op jit(solution)/shard_map/psum | solution.py:31
  443.8 0.8 multiply_reduce_fusion.1
  444.6 0.2 fusion.11
  444.8 62.2 %all-reduce = (f32[8,64]{1,0:T(8,128)S(1)}, f32[8]{0:T(128)S(1)}) all-reduce(f32[8,64]{1,0:T(8,128)S(1)} %bitcast.32, f32[8]{0:T(128)S(1)} %get-tuple-element.12), channel_id=1, replica_groups=mesh['ctx'=32,'cls'=8] {'ctx'}, use_global_device_ids=true, to_apply=%region_5.6 | all-reduce | flops 520 | bytes 4160 | tf_op jit(solution)/shard_map/psum | solution.py:41
  507.0 0.7 divide_subtract_fusion
  507.7 0.1 fusion.18
  507.8 0.9 multiply_multiply_fusion
  508.7 56.1 %psum.39 = f32[8]{0:T(128)S(1)} all-reduce(f32[8]{0:T(128)S(1)} %get-tuple-element.11), channel_id=1, replica_groups=mesh['ctx'=32,'cls'=8] {'ctx'}, use_global_device_ids=true, to_apply=%region_9.10 | all-reduce | flops 8 | bytes 64 | tf_op jit(solution)/shard_map/psum | solution.py:55
  564.8 0.8 multiply_convert_fusion
  565.5 40.3 %all_gather.14 = bf16[64,256]{1,0:T(8,128)(2,1)} all-gather(bf16[8,256]{1,0:T(8,128)(2,1)S(1)} %multiply_convert_fusion), channel_id=1, replica_groups=mesh['ctx'=32,'cls'=8] {'cls'}, dimensions={0}, use_global_device_ids=true | all-gather | bytes 36864 | tf_op jit(solution)/shard_map/all_gather | solution.py:59
  605.8 0.2 reduce-scatter.3.cloned.1.call-start
  606.0 60.1 %all-gather.5.cloned.1.call-done = bf16[64,8192]{1,0:T(8,128)(2,1)} async-done(((bf16[64,256]{1,0:T(8,128)(2,1)}), bf16[64,8192]{1,0:T(8,128)(2,1)}) %all-gather.5.cloned.1.call-update) | async-done | bytes 1048592 | tf_op jit(solution)/shard_map/all_gather | solution.py:60
  666.2 17.7 %fusion.1 = f32[64,8192]{1,0:T(8,128)} fusion(bf16[768,8192]{1,0:T(8,128)(2,1)} %param.7, bf16[64,8192]{1,0:T(8,128)(2,1)} %all-gather.5.cloned.1.call-done, f32[64,768]{1,0:T(8,128)S(1)} %get-tuple-element.17, f32[64]{0:T(128)S(1)} %pmax.7, pred[768]{0:T(1024)(128)(4,1)S(1)} %add_compare_fusion), kind=kOutput, calls=%fused_computation.2 | convolution fusion | flops 1610809344 | bytes 15926272 | tf_op jit(solution)/shard_map/dot_general | solution.py:62
  683.9 0.0 reduce-scatter.5.cloned.1.call-start
  684.0 17.1 %psum.38 = f32[]{:T(128)} all-reduce(f32[]{:T(128)} %get-tuple-element.15), channel_id=1, replica_groups=mesh['ctx'=32,'cls'=8] {'cls'}, use_global_device_ids=true, to_apply=%region_7.8 | all-reduce | flops 1 | bytes 8 | tf_op jit(solution)/shard_map/psum | solution.py:46
  701.1 0.7 reshape.34
  701.8 195.9 %reduce-scatter.3.cloned.1.call-done = f32[64,256]{1,0:T(8,128)} async-done(((f32[64,8192]{1,0:T(8,128)}), f32[64,256]{1,0:T(8,128)}) %reduce-scatter.3.cloned.1.call-update) | async-done | bytes 65552 | tf_op jit(solution)/shard_map/reduce_scatter | solution.py:63
  897.7 0.1 broadcast_multiply_fusion
  897.8 1.0 copy.13
  899.5 35.1 %reduce-scatter.5.cloned.1.call-done = f32[8,256]{1,0:T(8,128)} async-done(((f32[64,256]{1,0:T(8,128)}), f32[8,256]{1,0:T(8,128)}) %reduce-scatter.5.cloned.1.call-update) | async-done | bytes 8208 | tf_op jit(solution)/shard_map/reduce_scatter | solution.py:64
  (16 shorter events, 0.1 us)
Async XLA Ops:
  7.2 84.7 %all-gather.3.cloned.1.call-start = ((), (), s32[]{:S(2)}) async-start(), calls=%async_computation.2 | async-start | bytes 1081344 | tf_op jit(solution)/shard_map/all_gather | solution.py:23
  24.1 419.7 %all-reduce.3.cloned.1.call-start = ((), (), s32[]{:S(2)}) async-start(), calls=%async_computation.3 | async-start | bytes 4194304 | tf_op jit(solution)/shard_map/psum | solution.py:31
  100.8 87.5 %copy-start = (bf16[256,512]{1,0:T(8,128)(2,1)S(1)}, bf16[256,512]{1,0:T(8,128)(2,1)}, u32[]{:S(2)}) copy-start(bf16[256,512]{1,0:T(8,128)(2,1)} %param.11) | copy-start | bytes 786436
  100.8 87.7 %copy-start.3 = (s32[512]{0:T(512)S(1)}, s32[512]{0:T(512)}, u32[]{:S(2)}) copy-start(s32[512]{0:T(512)} %param.13) | copy-start | bytes 6148
  100.8 87.7 %copy-start.2 = (f32[512]{0:T(512)S(1)}, f32[512]{0:T(512)}, u32[]{:S(2)}) copy-start(f32[512]{0:T(512)} %param.12) | copy-start | bytes 6148
  100.8 343.0 %copy-start.1 = (f32[256]{0:T(256)S(1)}, f32[256]{0:T(256)}, u32[]{:S(2)}) copy-start(f32[256]{0:T(256)} %param.10) | copy-start | bytes 3076
  188.2 477.9 %all-gather.5.cloned.1.call-start = ((), (), s32[]{:S(2)}) async-start(), calls=%async_computation.4 | async-start | bytes 1081344 | tf_op jit(solution)/shard_map/all_gather | solution.py:60
  605.8 291.9 %reduce-scatter.3.cloned.1.call-start = ((), (), s32[]{:S(2)}) async-start(), calls=%async_computation.5 | async-start | bytes 2162688 | tf_op jit(solution)/shard_map/reduce_scatter | solution.py:63
  683.9 250.6 %reduce-scatter.5.cloned.1.call-start = ((), (), s32[]{:S(2)}) async-start(), calls=%async_computation.6 | async-start | bytes 73728 | tf_op jit(solution)/shard_map/reduce_scatter | solution.py:64
Sparse Core Ops, SparseCore 0:
  24.2 67.5 all-gather.2
  188.4 255.4 all-reduce.2
  605.9 60.1 all-gather.4
  684.0 213.5 reduce-scatter.2
  900.7 33.7 reduce-scatter.4
where the time goes:
time: 944 us; the launch traced here: 942 us
  waiting for transfers between devices  613 us (65%)
  blocking collectives  272 us (29%)
  matrix products  35.2 us (4%)
  between operations  16.3 us (2%)
    psum x1, waiting for transfers between devices, shards(): whole_sum = lax.psum(pooled_part, ('ctx', 'cls'))  255 us
    reduce_scatter x1, waiting for transfers between devices, shards(): lax.psum_scatter(query_part, 'ctx', scatter_dimension=1, tiled=True)  196 us
    pmax x1, blocking collectives, shards(): peak = lax.pmax(local_peak, ('ctx', 'cls'))  79.1 us
    all_gather x1, waiting for transfers between devices, shards(): scores = project_add(lax.all_gather(query_block, 'ctx', axis=1, tiled=True))  67 us
    psum x1, blocking collectives, shards(): squares, logit_raw = lax.psum((square_part, logit_part), 'ctx')  62.2 us
    all_gather x1, waiting for transfers between devices, shards(): lax.all_gather(grad_block, 'ctx', axis=1, tiled=True)  60.1 us
    psum x1, blocking collectives, shards(): inner_mean = lax.psum(inner_part, 'ctx') / full_width  56.1 us
    all_gather x1, blocking collectives, shards(): grad_block = lax.all_gather(pooled_grad, 'cls', axis=0, tiled=True)  40.3 us
  transfers between devices with their start and end apart: 5, of which 5 were waited for; matrix products, arithmetic and copies ran while one was open for 0% of the time, Pallas kernels for 0%

commit v1 on v0

v1 whole, which is shorter than its diff:
```python
import jax
import jax.numpy as jnp
from jax import lax
from jax.experimental import pallas as pl
from jax.experimental.pallas import tpu as pltpu
from jax.sharding import PartitionSpec as P

MESH = pl.DeviceIdType.MESH
F32, BF16 = jnp.float32, jnp.bfloat16
NT = (((1,), (1,)), ((), ()))
TN = (((0,), (0,)), ((), ()))
SIDE, DEPTH = 4, 8
SPAN = 2048
FAR = -1e30
ORDER = (2, 1, 3, 0)


def kernel(
    doc_ref, tokens_hbm, query_ref, gain_ref, head_hbm, bias_ref, label_ref,
    loss_ref, query_grad_ref, head_grad_hbm, bias_grad_ref,
    tok, head, head_grad, gathered1, gathered2, rhs, scores, weights, lhs, total,
    pair_send1, pair_recv1, a_send1, a_recv1, b_send1, b_recv1,
    pair_send2, pair_recv2, a_send2, a_recv2, b_send2, b_recv2,
    peak_own, peak_pair, peak_a, peak_b, peak_send2, peak_send3, f_pair, f_a, f_b,
    part_send, part_recv, loss_send, loss_pair, loss_send2, loss_y,
    load_sem, gather_sems, gather_send, scatter_sems, scatter_send, peak_sems, peak_send, misc_sems, misc_send,
):
    ctx, cls = lax.axis_index("ctx"), lax.axis_index("cls")
    x, z = lax.div(ctx, DEPTH), lax.rem(ctx, DEPTH)
    y, c = lax.div(cls, 2), lax.rem(cls, 2)
    a = y + c * (x - y)
    b = x + c * (y - x)

    def at(dx=0, dy=0, dz=0):
        return (
            lax.rem(x + dx, SIDE) * DEPTH + lax.rem(z + dz, DEPTH),
            lax.rem(y + dy, SIDE) * 2 + c,
        )

    def on_a(d):
        return at(dx=d * c, dy=d * (1 - c))

    def on_b(d, dz):
        return at(dx=d * (1 - c), dy=d * c, dz=dz)

    partner = (ctx, y * 2 + 1 - c)
    plane = [(d, dz) for d in range(SIDE) for dz in range(DEPTH) if d or dz]

    def send(src, dst, send_sem, recv_sem, to):
        pltpu.make_async_remote_copy(
            src_ref=src, dst_ref=dst, send_sem=send_sem, recv_sem=recv_sem,
            device_id=to, device_id_type=MESH,
        ).start()

    def take(sem, ref):
        pltpu.make_async_copy(ref, ref, sem).wait()

    load_tok = pltpu.make_async_copy(tokens_hbm, tok, load_sem.at[0])
    load_head = pltpu.make_async_copy(head_hbm, head, load_sem.at[1])
    load_tok.start()
    load_head.start()

    barrier = pltpu.get_barrier_semaphore()

    def greet(to):
        pl.semaphore_signal(barrier, inc=1, device_id=to, device_id_type=MESH)

    for d, dz in plane:
        greet(on_b(d, dz))
    for d in range(1, SIDE):
        greet(on_a(d))
    greet(partner)

    @pl.when(c == 1)
    def _():
        for d, dz in plane:
            if d and dz:
                greet(at(dx=d, dz=dz))

    pl.semaphore_wait(barrier, 35 + 21 * c)

    def split(rows):
        return jnp.concatenate([rows[:, :128], rows[:, 128:]], axis=0)

    def gather_begin(g, p, rows):
        g[c, a, b, z] = split(rows).astype(BF16)
        own = g.at[c, a, b, z]
        for d, dz in plane:
            send(own, own, gather_send.at[p, 0], gather_sems.at[p, d], on_b(d, dz))

    def gather_spread(g, p):
        for d in (0, 1, 3, 2):
            unit = g.at[c, a, lax.rem(b + SIDE - d, SIDE)]
            take(gather_sems.at[p, d], unit.at[pl.ds(0, 7)] if d == 0 else unit)
            for e in range(1, SIDE):
                span = d + c * (e - d)
                send(unit, unit, gather_send.at[p, 1], gather_sems.at[p, 4 + span], on_a(e))

    def gather_forward(g, p, j):
        at_x = lax.rem(x + SIDE - j, SIDE)

        @pl.when(c == 0)
        def _():
            take(gather_sems.at[p, 4 + j], g.at[0, 0, pl.ds(0, 3)])
            part = g.at[0, :, at_x]
            send(part, part, gather_send.at[p, 2], gather_sems.at[p, 8 + j], partner)

        @pl.when(c == 1)
        def _():
            if j:
                take(gather_sems.at[p, 4 + j], g.at[0, 0])
            part = g.at[1, at_x]
            send(part, part, gather_send.at[p, 2], gather_sems.at[p, 8 + j], partner)

    def project(g, p, j, first):
        at_x = lax.rem(x + SIDE - j, SIDE)
        take(gather_sems.at[p, 8 + j], g.at[0, 0])
        for zz in range(DEPTH):
            for yy in range(SIDE):
                even = g[0, yy, at_x, zz].astype(F32)
                odd = g[1, at_x, yy, zz].astype(F32)
                for half in range(2):
                    rows = slice(8 * half, 8 * half + 8)
                    col = 256 * zz + 128 * half
                    rhs[16 * yy : 16 * yy + 16, col : col + 128] = jnp.concatenate(
                        [even[rows], odd[rows]], axis=0
                    ).astype(BF16)
        cols = pl.ds(pl.multiple_of(at_x * SPAN, SPAN), SPAN)
        more = lax.dot_general(tok[:, cols], rhs[...], NT, preferred_element_type=F32)
        if first:
            scores[...] = more
        else:
            scores[...] += more

    def gather_project(g, p):
        gather_spread(g, p)
        ready = (0, 1, 3, 2)
        gather_forward(g, p, ready[0])
        for n in range(SIDE):
            if n + 1 < SIDE:
                gather_forward(g, p, ready[n + 1])
            project(g, p, ready[n], n == 0)

    def pair_begin(p, j, pair_send, pair_recv):
        cols = pl.ds(pl.multiple_of(lax.rem(x + j, SIDE) * SPAN, SPAN), SPAN)
        total[j] = jnp.dot(lhs[...], tok[:, cols], preferred_element_type=F32)
        for yy in range(SIDE):
            rows = pl.ds(pl.multiple_of(16 * yy + 8 * (1 - c), 8), 8)
            for zz in range(DEPTH):
                col = 256 * zz
                pair_send[j, yy, zz] = jnp.concatenate(
                    [total[j, rows, col : col + 128], total[j, rows, col + 128 : col + 256]], axis=0
                ).astype(BF16)
        send(pair_send.at[j], pair_recv.at[j], scatter_send.at[p, 0], scatter_sems.at[p, j], partner)

    def pair_end(p, j, pair_recv, a_send, a_recv, scaled):
        take(scatter_sems.at[p, j], pair_recv.at[j])
        for i in range(SIDE):
            yy = lax.rem(y + i, SIDE)
            rows = pl.ds(pl.multiple_of(16 * yy + 8 * c, 8), 8)
            for zz in range(DEPTH):
                col = 256 * zz
                came = pair_recv[j, yy, zz].astype(F32)
                lo, hi = total[j, rows, col : col + 128], total[j, rows, col + 128 : col + 256]
                if scaled:
                    mine, theirs = f_pair[0, rows], f_pair[1, rows]
                    lo, hi = lo * mine + came[:8] * theirs, hi * mine + came[8:] * theirs
                else:
                    lo, hi = lo + came[:8], hi + came[8:]
                a_send[j, i, zz] = jnp.concatenate([lo, hi], axis=0).astype(BF16)

        @pl.when(c == 0)
        def _():
            for i in range(1, SIDE):
                send(a_send.at[j, i], a_recv.at[i - 1, j], scatter_send.at[p, 1], scatter_sems.at[p, 4 + j], on_a(i))

        if j:

            @pl.when(c == 1)
            def _():
                send(a_send.at[j], a_recv.at[j - 1], scatter_send.at[p, 1], scatter_sems.at[p, 4 + j], on_a(j))

    def a_end(p, u, a_send, a_recv, b_send, b_recv, scaled):
        @pl.when(c == 0)
        def _():
            take(scatter_sems.at[p, 4 + u], a_recv.at[0, pl.ds(0, 3)])

        if u == ORDER[0]:

            @pl.when(c == 1)
            def _():
                for j in range(1, SIDE):
                    take(scatter_sems.at[p, 4 + j], a_recv.at[0])

        rows = pl.ds(pl.multiple_of(16 * lax.rem(y + c * u, SIDE) + 8 * c, 8), 8)
        for zz in range(DEPTH):
            parts = [a_send[u * (1 - c), u * c, zz]] + [a_recv[k, u, zz] for k in range(3)]
            lo = hi = None
            for k, part in enumerate(parts):
                part = part.astype(F32)
                low, high = part[:8], part[8:]
                if scaled:
                    factor = f_a[k, rows]
                    low, high = low * factor, high * factor
                lo, hi = (low, high) if lo is None else (lo + low, hi + high)
            b_send[u, zz] = jnp.concatenate([lo, hi], axis=0).astype(BF16)
        for dz in range(DEPTH):
            if u or dz:
                send(
                    b_send.at[u, lax.rem(z + dz, DEPTH)], b_recv.at[u * DEPTH + dz],
                    scatter_send.at[p, 2], scatter_sems.at[p, 8], on_b(u, dz),
                )

    def b_end(p, b_send, b_recv, scaled):
        take(scatter_sems.at[p, 8], b_recv.at[pl.ds(1, 31)])
        lo = hi = None
        for k in range(SIDE * DEPTH):
            part = (b_recv[k] if k else b_send[0, z]).astype(F32)
            low, high = part[:8], part[8:]
            if scaled:
                factor = f_b[k]
                low, high = low * factor, high * factor
            lo, hi = (low, high) if lo is None else (lo + low, hi + high)
        return jnp.concatenate([lo, hi], axis=1)

    def as_column(row):
        wide = jnp.concatenate([row] * 8, axis=0)
        lane = lax.broadcasted_iota(jnp.int32, (64, 128), 1)
        sub = lax.broadcasted_iota(jnp.int32, (64, 128), 0)
        column = jnp.sum(jnp.where(lane == sub, wide, 0.0), axis=1, keepdims=True)
        return jnp.broadcast_to(column, (64, 128))

    rhs[64:, :] = jnp.zeros((64, SPAN), BF16)
    gather_begin(gathered1, 0, query_ref[...].astype(F32))
    load_tok.wait()
    gather_project(gathered1, 0)

    count = tok.shape[0]
    place = (ctx * 8 + cls) * count + lax.broadcasted_iota(jnp.int32, (count, 128), 0)
    valid = place < doc_ref[0]
    masked = jnp.where(valid, scores[...], FAR)
    peak = jnp.max(masked, axis=0, keepdims=True)
    peak_own[...] = jnp.broadcast_to(peak, (8, 128))
    send(peak_own, peak_pair, peak_send.at[0], peak_sems.at[0], partner)
    soft = jnp.where(valid, jnp.exp(masked - peak), 0.0)
    weights[...] = soft
    lhs[...] = soft.T[:64].astype(BF16)

    first = (0, pair_send1, pair_recv1)
    pair_begin(0, ORDER[0], pair_send1, pair_recv1)
    take(peak_sems.at[0], peak_pair)
    peak2 = jnp.maximum(peak_own[...], peak_pair[...])
    peak_send2[...] = peak2
    for d in range(1, SIDE):
        send(peak_send2, peak_a.at[d - 1], peak_send.at[1], peak_sems.at[1], on_a(d))
    f_pair[0] = as_column(jnp.exp(peak_own[...] - peak2))
    f_pair[1] = as_column(jnp.exp(peak_pair[...] - peak2))
    for n in range(1, SIDE):
        pair_begin(0, ORDER[n], pair_send1, pair_recv1)
        pair_end(0, ORDER[n - 1], pair_recv1, a_send1, a_recv1, True)
    pair_end(0, ORDER[-1], pair_recv1, a_send1, a_recv1, True)
    take(peak_sems.at[1], peak_a)
    peak3 = peak_send2[...]
    for k in range(3):
        peak3 = jnp.maximum(peak3, peak_a[k])
    peak_send3[...] = peak3
    for d, dz in plane:
        send(peak_send3, peak_b.at[d * DEPTH + dz], peak_send.at[2], peak_sems.at[2], on_b(d, dz))
    f_a[0] = as_column(jnp.exp(peak_send2[...] - peak3))
    for k in range(3):
        f_a[k + 1] = as_column(jnp.exp(peak_a[k] - peak3))
    for u in ORDER:
        a_end(0, u, a_send1, a_recv1, b_send1, b_recv1, True)
    take(peak_sems.at[2], peak_b.at[pl.ds(1, 31)])
    peak_b[0] = peak_send3[...]
    top = jnp.max(peak_b[...], axis=0)
    lane8 = lax.broadcasted_iota(jnp.int32, (8, 128), 1)
    row8 = lax.broadcasted_iota(jnp.int32, (8, 128), 0)
    here = lane8 == row8 + (16 * y + 8 * c)
    for k in range(SIDE * DEPTH):
        factor = jnp.sum(jnp.where(here, jnp.exp(peak_b[k] - top), 0.0), axis=1, keepdims=True)
        f_b[k] = jnp.broadcast_to(factor, (8, 128))
    pooled = b_end(0, b_send1, b_recv1, True)

    load_head.wait()
    gain = gain_ref[...]
    lane512 = lax.broadcasted_iota(jnp.int32, (8, 512), 1)
    row512 = lax.broadcasted_iota(jnp.int32, (8, 512), 0)
    mine = (lane512 >= row512 * 64) & (lane512 < row512 * 64 + 64)
    low_half = lane8 < 64
    even_row = (row8 & 1) == 0
    active = (low_half & even_row) | (~low_half & ~even_row)

    def fold(wide):
        wide = jnp.where(mine, wide, 0.0)
        return wide[:, :128] + wide[:, 128:256] + wide[:, 256:384] + wide[:, 384:]

    product = jnp.dot((pooled * gain).astype(BF16), head[...], preferred_element_type=F32)
    square = jnp.sum(pooled * pooled, axis=1, keepdims=True)
    part_send[...] = jnp.where(active, fold(product), square)
    for d, dz in plane:
        send(part_send, part_recv.at[ctx], misc_send.at[0], misc_sems.at[0], at(dx=d, dz=dz))
    part_recv[ctx] = part_send[...]
    bias = fold(jnp.broadcast_to(bias_ref[...], (8, 512)))
    target = fold(jnp.broadcast_to(label_ref[...].astype(F32), (8, 512)))
    take(misc_sems.at[0], part_recv.at[pl.ds(0, 31)])
    raw = jnp.sum(part_recv[...], axis=0)
    squares = jnp.max(jnp.where(active, FAR, raw), axis=1, keepdims=True)
    inverse = lax.rsqrt(squares / (SPAN * SIDE) + 1e-05)
    logits = inverse * raw + bias
    grad = jnp.where(active, jax.nn.sigmoid(logits) - target, 0.0)
    inner = inverse * jnp.sum(jnp.where(active, grad * raw, 0.0), axis=1, keepdims=True) / (SPAN * SIDE)
    wide = jnp.where(mine, jnp.concatenate([grad] * 4, axis=1), 0.0)
    wide_hi = wide.astype(BF16).astype(F32)
    wide_lo = wide - wide_hi
    back = lax.dot_general(
        jnp.concatenate([wide_hi, wide_lo], axis=0).astype(BF16), head[...], NT, preferred_element_type=F32
    )
    normed_grad = (back[:8] + back[8:]) * gain
    unit = pooled * inverse
    pooled_grad = inverse * (normed_grad - unit * inner)

    gather_begin(gathered2, 1, pooled_grad)
    bias_grad_ref[...] = jnp.sum(wide, axis=0, keepdims=True)
    soft_plus = jnp.maximum(logits, 0.0) + jnp.log1p(jnp.exp(-jnp.abs(logits)))
    loss = jnp.where(active, soft_plus - target * logits, 0.0)
    loss = jnp.sum(jnp.sum(loss, axis=1, keepdims=True), axis=0, keepdims=True)
    loss_send[...] = jnp.broadcast_to(loss, (8, 128))
    send(loss_send, loss_pair, misc_send.at[1], misc_sems.at[1], partner)
    normed = unit * gain
    normed_hi = normed.astype(BF16).astype(F32)
    none = jnp.zeros((8, 256), F32)
    left = jnp.concatenate([normed_hi, normed - normed_hi, normed_hi, none], axis=0).astype(BF16)
    right = jnp.concatenate([wide_hi, wide_hi, wide_lo, jnp.zeros((8, 512), F32)], axis=0).astype(BF16)
    head_grad[...] = lax.dot_general(left, right, TN, preferred_element_type=F32)
    store_head = pltpu.make_async_copy(head_grad, head_grad_hbm, load_sem.at[2])
    store_head.start()
    take(misc_sems.at[1], loss_pair)
    loss_send2[...] = loss_send[...] + loss_pair[...]
    for d in range(1, SIDE):
        send(loss_send2, loss_y.at[y], misc_send.at[2], misc_sems.at[2], at(dy=d))
    loss_y[y] = loss_send2[...]
    own_share = jnp.exp(peak_own[...] - top)[:1]
    weights[...] = weights[...] * own_share
    gather_project(gathered2, 1)
    lhs[...] = (weights[...] * scores[...]).T[:64].astype(BF16)

    pair_begin(1, ORDER[0], pair_send2, pair_recv2)
    for n in range(1, SIDE):
        pair_begin(1, ORDER[n], pair_send2, pair_recv2)
        pair_end(1, ORDER[n - 1], pair_recv2, a_send2, a_recv2, False)
    pair_end(1, ORDER[-1], pair_recv2, a_send2, a_recv2, False)
    for u in ORDER:
        a_end(1, u, a_send2, a_recv2, b_send2, b_recv2, False)
    take(misc_sems.at[2], loss_y.at[pl.ds(0, 3)])
    loss_ref[...] = jnp.sum(loss_y[...], axis=0) / 4096.0

    for p, (g, pair_recv, a_recv, b_recv) in enumerate(
        ((gathered1, pair_recv1, a_recv1, b_recv1), (gathered2, pair_recv2, a_recv2, b_recv2))
    ):
        take(gather_send.at[p, 0], b_recv.at[pl.ds(0, 31)])
        take(gather_send.at[p, 1], g.at[0, pl.ds(0, 3)])
        take(gather_send.at[p, 2], g.at[0])
        take(scatter_send.at[p, 0], pair_recv)
        take(scatter_send.at[p, 1], a_recv)
        take(scatter_send.at[p, 2], b_recv.at[pl.ds(0, 31)])
    take(peak_send.at[0], peak_pair)
    take(peak_send.at[1], peak_a)
    take(peak_send.at[2], peak_b.at[pl.ds(0, 31)])
    take(misc_send.at[0], part_recv.at[pl.ds(0, 31)])
    take(misc_send.at[1], loss_pair)
    take(misc_send.at[2], loss_y.at[pl.ds(0, 3)])
    store_head.wait()
    query_grad_ref[...] = b_end(1, b_send2, b_recv2, False)


def shards(tokens, doc_length, queries, norm_gain, head_weight, head_bias, labels):
    count, width = tokens.shape
    rows, features = queries.shape
    attributes = head_bias.shape[0]
    vmem = pl.BlockSpec(memory_space=pltpu.VMEM)
    anywhere = pl.BlockSpec(memory_space=pl.ANY)
    tile, row = (16, 128), (8, 128)

    def exchange():
        return [
            pltpu.VMEM((SIDE, SIDE, DEPTH, *tile), BF16),
            pltpu.VMEM((SIDE, SIDE, DEPTH, *tile), BF16),
            pltpu.VMEM((SIDE, SIDE, DEPTH, *tile), BF16),
            pltpu.VMEM((SIDE - 1, SIDE, DEPTH, *tile), BF16),
            pltpu.VMEM((SIDE, DEPTH, *tile), BF16),
            pltpu.VMEM((SIDE * DEPTH, *tile), BF16),
        ]

    loss, query_grad, head_grad, bias_grad = pl.pallas_call(
        kernel,
        out_shape=(
            jax.ShapeDtypeStruct(row, F32),
            jax.ShapeDtypeStruct((rows, features), F32),
            jax.ShapeDtypeStruct(head_weight.shape, F32),
            jax.ShapeDtypeStruct((1, attributes), F32),
        ),
        in_specs=[
            pl.BlockSpec(memory_space=pltpu.SMEM),
            anywhere,
            vmem,
            vmem,
            anywhere,
            vmem,
            vmem,
        ],
        out_specs=(vmem, vmem, anywhere, vmem),
        scratch_shapes=[
            pltpu.VMEM((count, width), BF16),
            pltpu.VMEM(head_weight.shape, BF16),
            pltpu.VMEM(head_weight.shape, F32),
            pltpu.VMEM((2, SIDE, SIDE, DEPTH, *tile), BF16),
            pltpu.VMEM((2, SIDE, SIDE, DEPTH, *tile), BF16),
            pltpu.VMEM((128, SPAN), BF16),
            pltpu.VMEM((count, 128), F32),
            pltpu.VMEM((count, 128), F32),
            pltpu.VMEM((64, count), BF16),
            pltpu.VMEM((SIDE, 64, SPAN), F32),
            *exchange(),
            *exchange(),
            pltpu.VMEM(row, F32),
            pltpu.VMEM(row, F32),
            pltpu.VMEM((SIDE - 1, *row), F32),
            pltpu.VMEM((SIDE * DEPTH, *row), F32),
            pltpu.VMEM(row, F32),
            pltpu.VMEM(row, F32),
            pltpu.VMEM((2, 64, 128), F32),
            pltpu.VMEM((SIDE, 64, 128), F32),
            pltpu.VMEM((SIDE * DEPTH, *row), F32),
            pltpu.VMEM(row, F32),
            pltpu.VMEM((SIDE * DEPTH, *row), F32),
            pltpu.VMEM(row, F32),
            pltpu.VMEM(row, F32),
            pltpu.VMEM(row, F32),
            pltpu.VMEM((SIDE, *row), F32),
            pltpu.SemaphoreType.DMA((3,)),
            pltpu.SemaphoreType.DMA((2, 12)),
            pltpu.SemaphoreType.DMA((2, 3)),
            pltpu.SemaphoreType.DMA((2, 9)),
            pltpu.SemaphoreType.DMA((2, 3)),
            pltpu.SemaphoreType.DMA((3,)),
            pltpu.SemaphoreType.DMA((3,)),
            pltpu.SemaphoreType.DMA((3,)),
            pltpu.SemaphoreType.DMA((3,)),
        ],
        compiler_params=pltpu.CompilerParams(
            collective_id=0, has_side_effects=True, vmem_limit_bytes=52 * 2**20
        ),
        name="pooling_step",
    )(
        doc_length,
        tokens,
        queries,
        norm_gain.reshape(1, -1),
        head_weight,
        head_bias.reshape(1, -1),
        labels.reshape(1, -1),
    )
    return loss[0, 0], query_grad, head_grad, bias_grad.reshape(-1)


def solution(mesh):
    return jax.shard_map(
        shards,
        mesh=mesh,
        in_specs=(
            P(("ctx", "cls"), None),
            P(),
            P("cls", "ctx"),
            P("ctx"),
            P("ctx", "cls"),
            P("cls"),
            P("cls"),
        ),
        out_specs=(P(), P("cls", "ctx"), P("ctx", "cls"), P("cls")),
        check_vma=False,
    )
```

time: 944 us -> 89.6 us (0.09)
  waiting for transfers between devices: 613 us -> 0 us
  blocking collectives: 272 us -> 0 us
  Pallas kernels: 0 us -> 81.8 us
  matrix products: 35.2 us -> 0 us
  between operations: 16.3 us -> 1.3 us
    psum x1 -> x0, waiting for transfers between devices: 255 us -> none  [shards(): whole_sum = lax.psum(pooled_part, ('ctx', 'cls'))]
    reduce_scatter x2 -> x0, waiting for transfers between devices: 231 us -> none  [the longest x1 196 us: shards(): lax.psum_scatter(query_part, 'ctx', scatter_dimension=1, tiled=True)]
    psum x3 -> x0, blocking collectives: 135 us -> none  [the longest x1 62.2 us: shards(): squares, logit_raw = lax.psum((square_part, logit_part), 'ctx')]
    all_gather x2 -> x0, waiting for transfers between devices: 127 us -> none  [the longest x1 67 us: shards(): scores = project_add(lax.all_gather(query_block, 'ctx', axis=1, tiled=True))]
    pallas_call x0 -> x1, Pallas kernels: none -> 81.8 us  [shards(): pl.pallas_call(kernel, out_shape=(jax.ShapeDtypeStruct(row, F32), jax.Sha...]
    pmax x1 -> x0, blocking collectives: 79.1 us -> none  [shards(): peak = lax.pmax(local_peak, ('ctx', 'cls'))]
    all_gather x2 -> x0, blocking collectives: 57.1 us -> none  [the longest x1 40.3 us: shards(): grad_block = lax.all_gather(pooled_grad, 'cls', axis=0, tiled=True)]
    dot_general x5 -> x0, matrix products: 35.2 us -> none  [the longest x1 17.7 us: shards(): query_part = jnp.dot(score_grad, tokens, preferred_element_type=jnp.float32)]
  transfers between devices with their start and end apart: 5 -> 0, of which waited for: 5 -> 0; matrix products, arithmetic and copies ran while one was open for 0% -> 0% of each run, Pallas kernels for 0% -> 0%
where the time goes in v1:
time: 89.6 us; the launch traced here: 89.2 us
  Pallas kernels  81.8 us (91%)
  local copies, waits for them, and re-layouts  6.15 us (7%)
  between operations  1.3 us (1%)
    pallas_call x1, Pallas kernels, shards(): pl.pallas_call(kernel, out_shape=(jax.ShapeDtypeStruct(row, F32), jax.Sha...  81.8 us
    unnamed x13, local copies, waits for them, and re-layouts  5.64 us

profile of v1, /device:TPU:1, one launch (start us, length us, event | category | flops | bytes accessed | tf_op | source)
XLA Modules:
  0.0 89.2 jit_solution(6564961602174600594)
XLA Ops:
  1.3 0.0 copy-start
  1.3 0.9 %copy-done = bf16[256,512]{1,0:T(8,128)(2,1)S(1)} copy-done((bf16[256,512]{1,0:T(8,128)(2,1)S(1)}, bf16[256,512]{1,0:T(8,128)(2,1)}, u32[]{:S(2)}) %copy-start) | copy-done | bytes 262168
  2.2 0.0 copy-start.1
  2.2 0.7 copy-done.1
  2.9 0.0 copy-start.2
  2.9 0.7 copy-done.2
  3.6 0.0 copy-start.3
  3.6 0.7 copy-done.3
  4.3 0.0 copy-start.4
  4.3 0.7 copy-done.4
  5.0 81.8 %pooling_step.1 = (f32[8,128]{1,0:T(8,128)S(1)}, f32[8,256]{1,0:T(8,128)S(1)}, f32[256,512]{1,0:T(8,128)S(1)}, f32[1,512]{1,0:T(1,128)S(1)}) custom-call(s32[1]{0:T(128)S(6)} %copy.14.doc_ref, bf16[768,8192]{1,0:T(8,128)(2,1)} %tokens_hbm.1, bf16[8,256]{1,0:T(8,128)(2,1)S(1)} %copy-done.1, f32[1,256]{1,0:T(1,128)S(1)} %bitcast.8, ...), custom_call_target="tpu_custom_call" | custom-call | tf_op jit(solution)/shard_map/pooling_step/pallas_call | solution.py:395
  86.8 0.5 slice.3
  87.3 0.6 copy.15
  87.9 0.8 copy.16
  88.7 0.6 copy.17
Async XLA Ops:
  1.3 1.0 %copy-start = (bf16[256,512]{1,0:T(8,128)(2,1)S(1)}, bf16[256,512]{1,0:T(8,128)(2,1)}, u32[]{:S(2)}) copy-start(bf16[256,512]{1,0:T(8,128)(2,1)} %head_hbm.1) | copy-start | bytes 786436
  2.2 0.7 copy-start.1
  2.9 0.7 copy-start.2
  3.6 0.7 copy-start.3
  4.3 0.7 copy-start.4

commit v2 on v1

v2 whole, which is shorter than its diff:
```python
import jax
import jax.numpy as jnp
from jax import lax
from jax.experimental import pallas as pl
from jax.experimental.pallas import tpu as pltpu
from jax.sharding import PartitionSpec as P

MESH = pl.DeviceIdType.MESH
F32, BF16 = jnp.float32, jnp.bfloat16
NT = (((1,), (1,)), ((), ()))
TN = (((0,), (0,)), ((), ()))
SIDE, DEPTH = 4, 8
SPAN = 2048
FAR = -1e30
ORDER = (2, 1, 3, 0)
READY = (0, 1, 3, 2)


def hops(d, dz):
    return min(d, SIDE - d) + min(dz, DEPTH - dz)


def kernel(
    doc_ref, tokens_hbm, query_hbm, gain_hbm, head_hbm, bias_hbm, label_hbm,
    loss_ref, query_grad_ref, normed_ref, wide_ref,
    tok, head, query_ref, gain_ref, bias_ref, label_ref, gathered1, gathered2, rhs, scores, weights, lhs, total,
    pair_send1, pair_recv1, a_send1, a_recv1, b_send1, b_recv1,
    pair_send2, pair_recv2, a_send2, a_recv2, b_send2, b_recv2,
    peak_own, peak_pair, peak_a, peak_b, peak_send2, peak_send3, f_pair, f_a, f_b,
    part_send, part_recv, loss_send, loss_pair, loss_send2, loss_y,
    load_sem, gather_sems, gather_send, scatter_sems, scatter_send, peak_sems, peak_send, misc_sems, misc_send,
):
    ctx, cls = lax.axis_index("ctx"), lax.axis_index("cls")
    x, z = ctx >> 3, ctx & 7
    y, c = cls >> 1, cls & 1
    a = y + c * (x - y)
    b = x + c * (y - x)

    x_at = [((x + d) & 3) * DEPTH for d in range(SIDE)]
    y_at = [((y + d) & 3) * 2 + c for d in range(SIDE)]
    z_at = [(z + d) & 7 for d in range(DEPTH)]
    x_if_b = [x_at[d] + c * (x_at[0] - x_at[d]) for d in range(SIDE)]
    y_if_b = [y_at[0] + c * (y_at[d] - y_at[0]) for d in range(SIDE)]
    x_if_a = [x_at[0] + c * (x_at[d] - x_at[0]) for d in range(SIDE)]
    y_if_a = [y_at[d] + c * (y_at[0] - y_at[d]) for d in range(SIDE)]

    def at(dx=0, dy=0, dz=0):
        return (x_at[dx] + z_at[dz], y_at[dy])

    def on_a(d):
        return (x_if_a[d] + z, y_if_a[d])

    def on_b(d, dz):
        return (x_if_b[d] + z_at[dz], y_if_b[d])

    partner = (ctx, y * 2 + 1 - c)
    plane = [(d, dz) for d in range(SIDE) for dz in range(DEPTH) if d or dz]
    plane.sort(key=lambda step: -hops(*step))

    def send(src, dst, send_sem, recv_sem, to):
        pltpu.make_async_remote_copy(
            src_ref=src, dst_ref=dst, send_sem=send_sem, recv_sem=recv_sem,
            device_id=to, device_id_type=MESH,
        ).start()

    def take(sem, ref):
        pltpu.make_async_copy(ref, ref, sem).wait()

    load_tok = pltpu.make_async_copy(tokens_hbm, tok, load_sem.at[0])
    load_query = pltpu.make_async_copy(query_hbm, query_ref, load_sem.at[1])
    load_rest = [
        pltpu.make_async_copy(src, dst, load_sem.at[2 + k])
        for k, (src, dst) in enumerate(
            ((head_hbm, head), (gain_hbm, gain_ref), (bias_hbm, bias_ref), (label_hbm, label_ref))
        )
    ]
    load_query.start()
    load_tok.start()
    for load in load_rest:
        load.start()

    barrier = pltpu.get_barrier_semaphore()

    def greet(to):
        pl.semaphore_signal(barrier, inc=1, device_id=to, device_id_type=MESH)

    for d, dz in plane:
        greet(on_b(d, dz))
    for d in range(1, SIDE):
        greet(on_a(d))
    greet(partner)

    pl.semaphore_wait(barrier, 35)

    def split(rows):
        return jnp.concatenate([rows[:, :128], rows[:, 128:]], axis=0)

    def gather_begin(g, p, rows):
        g[c, a, b, z] = split(rows).astype(BF16)
        own = g.at[c, a, b, z]
        for d, dz in sorted(plane, key=lambda step: (READY.index(step[0]), -hops(*step))):
            send(own, own, gather_send.at[p, 0], gather_sems.at[p, d], on_b(d, dz))

    def gather_spread(g, p):
        for d in READY:
            unit = g.at[c, a, (b + SIDE - d) & 3]
            take(gather_sems.at[p, d], unit.at[pl.ds(0, 7)] if d == 0 else unit)

            @pl.when(c == 0)
            def _():
                for e in (2, 1, 3):
                    send(unit, unit, gather_send.at[p, 2], gather_sems.at[p, 4 + d], on_a(e))

            @pl.when(c == 1)
            def _():
                for e in (1, 3, 2):
                    send(unit, unit, gather_send.at[p, 2], gather_sems.at[p, 4 + e], on_a(e))

    def gather_sent(g, p):
        take(gather_send.at[p, 0], b_recv1.at[pl.ds(0, 31)])
        take(gather_send.at[p, 1], g.at[0])
        take(gather_send.at[p, 2], g.at[0, pl.ds(0, 3)])

    def gather_forward(g, p, core, j):
        at_x = (x + SIDE - j) & 3

        @pl.when(c == core)
        def _():
            if core == 0:
                take(gather_sems.at[p, 4 + j], g.at[0, 0, pl.ds(0, 3)])
                part = g.at[0, :, at_x]
            else:
                if j:
                    take(gather_sems.at[p, 4 + j], g.at[0, 0])
                part = g.at[1, at_x]
            send(part, part, gather_send.at[p, 1], gather_sems.at[p, 8 + j], partner)

    def project(g, p, j, first):
        at_x = ((x + SIDE - j) & 3)
        take(gather_sems.at[p, 8 + j], g.at[0, 0])
        for zz in range(DEPTH):
            for yy in range(SIDE):
                even = g[0, yy, at_x, zz].astype(F32)
                odd = g[1, at_x, yy, zz].astype(F32)
                for half in range(2):
                    rows = slice(8 * half, 8 * half + 8)
                    col = 256 * zz + 128 * half
                    rhs[16 * yy : 16 * yy + 16, col : col + 128] = jnp.concatenate(
                        [even[rows], odd[rows]], axis=0
                    ).astype(BF16)
        cols = pl.ds(pl.multiple_of(at_x * SPAN, SPAN), SPAN)
        more = lax.dot_general(tok[:, cols], rhs[...], NT, preferred_element_type=F32)
        if first:
            scores[...] = more
        else:
            scores[...] += more

    def gather_project(g, p):
        gather_spread(g, p)
        gather_forward(g, p, 0, READY[0])
        gather_forward(g, p, 1, READY[0])
        for n, j in enumerate(READY):
            if n < 3:
                gather_forward(g, p, 0, READY[n + 1])
            if n in (1, 2):
                gather_forward(g, p, 1, READY[n + 1])
            project(g, p, j, n == 0)
            if n == 0:
                gather_forward(g, p, 1, READY[1])

    def pair_begin(p, j, pair_send, pair_recv):
        cols = pl.ds(pl.multiple_of(((x + j) & 3) * SPAN, SPAN), SPAN)
        total[j] = jnp.dot(lhs[...], tok[:, cols], preferred_element_type=F32)
        for yy in range(SIDE):
            rows = pl.ds(pl.multiple_of(16 * yy + 8 * (1 - c), 8), 8)
            for zz in range(DEPTH):
                col = 256 * zz
                pair_send[j, yy, zz] = jnp.concatenate(
                    [total[j, rows, col : col + 128], total[j, rows, col + 128 : col + 256]], axis=0
                ).astype(BF16)
        send(pair_send.at[j], pair_recv.at[j], scatter_send.at[p, 0], scatter_sems.at[p, j], partner)

    def pair_end(p, j, pair_recv, a_send, a_recv, scaled):
        take(scatter_sems.at[p, j], pair_recv.at[j])
        for i in range(SIDE):
            yy = ((y + i) & 3)
            rows = pl.ds(pl.multiple_of(16 * yy + 8 * c, 8), 8)
            for zz in range(DEPTH):
                col = 256 * zz
                came = pair_recv[j, yy, zz].astype(F32)
                lo, hi = total[j, rows, col : col + 128], total[j, rows, col + 128 : col + 256]
                if scaled:
                    mine, theirs = f_pair[0, rows], f_pair[1, rows]
                    lo, hi = lo * mine + came[:8] * theirs, hi * mine + came[8:] * theirs
                else:
                    lo, hi = lo + came[:8], hi + came[8:]
                a_send[j, i, zz] = jnp.concatenate([lo, hi], axis=0).astype(BF16)

        @pl.when(c == 0)
        def _():
            for i in range(1, SIDE):
                send(a_send.at[j, i], a_recv.at[i - 1, j], scatter_send.at[p, 1], scatter_sems.at[p, 4 + j], on_a(i))

        if j:

            @pl.when(c == 1)
            def _():
                send(a_send.at[j], a_recv.at[j - 1], scatter_send.at[p, 1], scatter_sems.at[p, 4 + j], on_a(j))

    def a_end(p, u, a_send, a_recv, b_send, b_recv, scaled):
        @pl.when(c == 0)
        def _():
            take(scatter_sems.at[p, 4 + u], a_recv.at[0, pl.ds(0, 3)])

        if u == ORDER[0]:

            @pl.when(c == 1)
            def _():
                for j in range(1, SIDE):
                    take(scatter_sems.at[p, 4 + j], a_recv.at[0])

        rows = pl.ds(pl.multiple_of(16 * ((y + c * u) & 3) + 8 * c, 8), 8)
        for zz in range(DEPTH):
            parts = [a_send[u * (1 - c), u * c, zz]] + [a_recv[k, u, zz] for k in range(3)]
            lo = hi = None
            for k, part in enumerate(parts):
                part = part.astype(F32)
                low, high = part[:8], part[8:]
                if scaled:
                    factor = f_a[k, rows]
                    low, high = low * factor, high * factor
                lo, hi = (low, high) if lo is None else (lo + low, hi + high)
            b_send[u, zz] = jnp.concatenate([lo, hi], axis=0).astype(BF16)
        for dz in sorted(range(DEPTH), key=lambda dz: -hops(u, dz)):
            if u or dz:
                send(
                    b_send.at[u, z_at[dz]], b_recv.at[u * DEPTH + dz],
                    scatter_send.at[p, 2], scatter_sems.at[p, 8], on_b(u, dz),
                )

    def b_end(p, b_send, b_recv, scaled):
        take(scatter_sems.at[p, 8], b_recv.at[pl.ds(1, 31)])
        lo = hi = None
        for k in range(SIDE * DEPTH):
            part = (b_recv[k] if k else b_send[0, z]).astype(F32)
            low, high = part[:8], part[8:]
            if scaled:
                factor = f_b[k]
                low, high = low * factor, high * factor
            lo, hi = (low, high) if lo is None else (lo + low, hi + high)
        return jnp.concatenate([lo, hi], axis=1)

    def as_column(row):
        wide = jnp.broadcast_to(row, (64, 128))
        lane = lax.broadcasted_iota(jnp.int32, (64, 128), 1)
        sub = lax.broadcasted_iota(jnp.int32, (64, 128), 0)
        column = jnp.sum(jnp.where(lane == sub, wide, 0.0), axis=1, keepdims=True)
        return jnp.broadcast_to(column, (64, 128))

    rhs[64:, :] = jnp.zeros((64, SPAN), BF16)
    load_query.wait()
    gather_begin(gathered1, 0, query_ref[...].astype(F32))
    load_tok.wait()
    gather_project(gathered1, 0)

    @pl.when(c == 1)
    def _():
        for d, dz in plane:
            if d and dz:
                greet(at(dx=d, dz=dz))

    count = tok.shape[0]
    place = (ctx * 8 + cls) * count + lax.broadcasted_iota(jnp.int32, (count, 128), 0)
    valid = place < doc_ref[0]
    masked = jnp.where(valid, scores[...], FAR)
    peak = jnp.max(masked, axis=0, keepdims=True)
    peak_own[...] = peak
    send(peak_own, peak_pair, peak_send.at[0], peak_sems.at[0], partner)
    soft = jnp.where(valid, jnp.exp(masked - peak), 0.0)
    weights[...] = soft
    lhs[...] = soft.T[:64].astype(BF16)

    first = (0, pair_send1, pair_recv1)
    pair_begin(0, ORDER[0], pair_send1, pair_recv1)
    take(peak_sems.at[0], peak_pair)
    peak2 = jnp.maximum(peak_own[...], peak_pair[...])
    peak_send2[...] = peak2
    for d in range(1, SIDE):
        send(peak_send2, peak_a.at[d - 1], peak_send.at[1], peak_sems.at[1], on_a(d))
    f_pair[0] = as_column(jnp.exp(peak_own[...] - peak2))
    f_pair[1] = as_column(jnp.exp(peak_pair[...] - peak2))
    for n in range(1, SIDE):
        pair_begin(0, ORDER[n], pair_send1, pair_recv1)
        pair_end(0, ORDER[n - 1], pair_recv1, a_send1, a_recv1, True)
    pair_end(0, ORDER[-1], pair_recv1, a_send1, a_recv1, True)
    take(peak_sems.at[1], peak_a)
    peak3 = peak_send2[...]
    for k in range(3):
        peak3 = jnp.maximum(peak3, peak_a[k])
    peak_send3[...] = peak3
    for d, dz in plane:
        send(peak_send3, peak_b.at[d * DEPTH + dz], peak_send.at[2], peak_sems.at[2], on_b(d, dz))
    f_a[0] = as_column(jnp.exp(peak_send2[...] - peak3))
    for k in range(3):
        f_a[k + 1] = as_column(jnp.exp(peak_a[k] - peak3))
    for u in ORDER:
        a_end(0, u, a_send1, a_recv1, b_send1, b_recv1, True)
    take(peak_sems.at[2], peak_b.at[pl.ds(1, 31)])
    peak_b[0] = peak_send3[...]
    top = peak_b[0]
    for k in range(1, SIDE * DEPTH):
        top = jnp.maximum(top, peak_b[k])
    lane8 = lax.broadcasted_iota(jnp.int32, (8, 128), 1)
    row8 = lax.broadcasted_iota(jnp.int32, (8, 128), 0)
    here = lane8 == row8 + (16 * y + 8 * c)
    for k in range(SIDE * DEPTH):
        factor = jnp.sum(jnp.where(here, jnp.broadcast_to(jnp.exp(peak_b[k] - top), (8, 128)), 0.0), axis=1, keepdims=True)
        f_b[k] = jnp.broadcast_to(factor, (8, 128))
    pooled = b_end(0, b_send1, b_recv1, True)

    for load in load_rest:
        load.wait()
    gain = gain_ref[...]
    lane512 = lax.broadcasted_iota(jnp.int32, (8, 512), 1)
    row512 = lax.broadcasted_iota(jnp.int32, (8, 512), 0)
    mine = (lane512 >= row512 * 64) & (lane512 < row512 * 64 + 64)
    diagonal = lane8 == row8

    def flat(wide):
        return jnp.sum(jnp.where(mine, wide, 0.0), axis=0, keepdims=True)

    product = flat(jnp.dot((pooled * gain).astype(BF16), head[...], preferred_element_type=F32))
    square = jnp.sum(pooled * pooled, axis=1, keepdims=True)
    square = jnp.sum(jnp.where(diagonal, square, 0.0), axis=0, keepdims=True)
    part_send[...] = jnp.concatenate([product[:, 128 * k : 128 * k + 128] for k in range(4)] + [square], axis=0)

    @pl.when(c == 1)
    def _():
        pl.semaphore_wait(barrier, 21)

    for d, dz in plane:
        send(part_send, part_recv.at[ctx], misc_send.at[0], misc_sems.at[0], at(dx=d, dz=dz))
    part_recv[ctx] = part_send[...]
    bias = bias_ref[...]
    target = label_ref[...].astype(F32)
    take(misc_sems.at[0], part_recv.at[pl.ds(0, 31)])
    whole = part_recv[0]
    for k in range(1, SIDE * DEPTH):
        whole = whole + part_recv[k]
    raw = jnp.concatenate([whole[k : k + 1] for k in range(4)], axis=1)
    squares = jnp.broadcast_to(whole[4:5], (8, 128))
    squares = jnp.sum(jnp.where(diagonal, squares, 0.0), axis=1, keepdims=True)
    inverse = lax.rsqrt(squares / (SPAN * SIDE) + 1e-05)
    logits = flat(jnp.broadcast_to(inverse, (8, 512))) * raw + bias
    grad = jax.nn.sigmoid(logits) - target
    wide = jnp.where(mine, jnp.broadcast_to(grad, (8, 512)), 0.0)
    inner = inverse * jnp.sum(wide * raw, axis=1, keepdims=True) / (SPAN * SIDE)
    wide_hi = wide.astype(BF16).astype(F32)
    wide_lo = wide - wide_hi
    back = lax.dot_general(
        jnp.concatenate([wide_hi, wide_lo], axis=0).astype(BF16), head[...], NT, preferred_element_type=F32
    )
    normed_grad = (back[:8] + back[8:]) * gain
    unit = pooled * inverse
    pooled_grad = inverse * (normed_grad - unit * inner)

    gather_begin(gathered2, 1, pooled_grad)
    normed_ref[...] = unit * gain
    wide_ref[...] = wide
    soft_plus = jnp.maximum(logits, 0.0) + jnp.log1p(jnp.exp(-jnp.abs(logits)))
    loss = jnp.sum(soft_plus - target * logits, axis=1, keepdims=True)
    loss_send[...] = jnp.broadcast_to(loss, (1, 128))
    send(loss_send, loss_pair, misc_send.at[1], misc_sems.at[1], partner)
    own_share = jnp.exp(peak_own[...] - top)
    weights[...] = weights[...] * own_share
    gather_project(gathered2, 1)
    take(misc_sems.at[1], loss_pair)
    loss_send2[...] = loss_send[...] + loss_pair[...]
    for d in range(1, SIDE):
        send(loss_send2, loss_y.at[y], misc_send.at[2], misc_sems.at[2], at(dy=d))
    loss_y[y] = loss_send2[...]
    lhs[...] = (weights[...] * scores[...]).T[:64].astype(BF16)

    pair_begin(1, ORDER[0], pair_send2, pair_recv2)
    for n in range(1, SIDE):
        pair_begin(1, ORDER[n], pair_send2, pair_recv2)
        pair_end(1, ORDER[n - 1], pair_recv2, a_send2, a_recv2, False)
    pair_end(1, ORDER[-1], pair_recv2, a_send2, a_recv2, False)
    for u in ORDER:
        a_end(1, u, a_send2, a_recv2, b_send2, b_recv2, False)
    take(misc_sems.at[2], loss_y.at[pl.ds(0, 3)])
    loss_ref[0, 0] = jnp.sum(loss_y[...], axis=0)[0, 0] / 4096.0

    for p, (g, pair_recv, a_recv, b_recv) in enumerate(
        ((gathered1, pair_recv1, a_recv1, b_recv1), (gathered2, pair_recv2, a_recv2, b_recv2))
    ):
        gather_sent(g, p)
        take(scatter_send.at[p, 0], pair_recv)
        take(scatter_send.at[p, 1], a_recv)
        take(scatter_send.at[p, 2], b_recv.at[pl.ds(0, 31)])
    take(peak_send.at[0], peak_pair)
    take(peak_send.at[1], peak_a)
    take(peak_send.at[2], peak_b.at[pl.ds(0, 31)])
    take(misc_send.at[0], part_recv.at[pl.ds(0, 31)])
    take(misc_send.at[1], loss_pair)
    take(misc_send.at[2], loss_y.at[pl.ds(0, 3)])
    query_grad_ref[...] = b_end(1, b_send2, b_recv2, False)


def deliver(
    wide_in, normed_in, query_in, loss_in, head_out, bias_out, query_out, loss_out,
    wide_ref, normed_ref, query_ref, loss_ref, head_ref, bias_ref, sems,
):
    pairs = ((wide_in, wide_ref), (normed_in, normed_ref), (query_in, query_ref), (loss_in, loss_ref))
    loads = [pltpu.make_async_copy(src, dst, sems.at[k]) for k, (src, dst) in enumerate(pairs)]
    pairs = ((head_ref, head_out), (bias_ref, bias_out), (query_ref, query_out), (loss_ref, loss_out))
    stores = [pltpu.make_async_copy(src, dst, sems.at[4 + k]) for k, (src, dst) in enumerate(pairs)]
    for load in loads:
        load.start()
    for k in (2, 3):
        loads[k].wait()
        stores[k].start()
    loads[0].wait()
    wide = wide_ref[...]
    bias_ref[...] = jnp.sum(wide, axis=0, keepdims=True)
    stores[1].start()
    loads[1].wait()
    normed = normed_ref[...]
    normed_hi, wide_hi = normed.astype(BF16).astype(F32), wide.astype(BF16).astype(F32)
    left = [normed_hi, normed - normed_hi, normed_hi, jnp.zeros_like(normed)]
    right = [wide_hi, wide_hi, wide - wide_hi, jnp.zeros_like(wide)]
    left, right = (jnp.concatenate(rows, axis=0).astype(BF16) for rows in (left, right))
    head_ref[...] = lax.dot_general(left, right, TN, preferred_element_type=F32)
    stores[0].start()
    for store in stores:
        store.wait()


def shards(tokens, doc_length, queries, norm_gain, head_weight, head_bias, labels):
    count, width = tokens.shape
    rows, features = queries.shape
    attributes = head_bias.shape[0]
    vmem = pl.BlockSpec(memory_space=pltpu.VMEM)
    hbm = pl.BlockSpec(memory_space=pltpu.HBM)
    tile, row = (16, 128), (8, 128)

    def exchange():
        return [
            pltpu.VMEM((SIDE, SIDE, DEPTH, *tile), BF16),
            pltpu.VMEM((SIDE, SIDE, DEPTH, *tile), BF16),
            pltpu.VMEM((SIDE, SIDE, DEPTH, *tile), BF16),
            pltpu.VMEM((SIDE - 1, SIDE, DEPTH, *tile), BF16),
            pltpu.VMEM((SIDE, DEPTH, *tile), BF16),
            pltpu.VMEM((SIDE * DEPTH, *tile), BF16),
        ]

    loss, query_grad, normed, wide = pl.pallas_call(
        kernel,
        out_shape=(
            jax.ShapeDtypeStruct((1, 1), F32),
            jax.ShapeDtypeStruct((rows, features), F32),
            jax.ShapeDtypeStruct((rows, features), F32),
            jax.ShapeDtypeStruct((rows, attributes), F32),
        ),
        in_specs=[
            pl.BlockSpec(memory_space=pltpu.SMEM),
            hbm,
            hbm,
            hbm,
            hbm,
            hbm,
            hbm,
        ],
        out_specs=(pl.BlockSpec(memory_space=pltpu.SMEM), vmem, vmem, vmem),
        scratch_shapes=[
            pltpu.VMEM((count, width), BF16),
            pltpu.VMEM(head_weight.shape, BF16),
            pltpu.VMEM(queries.shape, BF16),
            pltpu.VMEM((1, features), F32),
            pltpu.VMEM((1, attributes), F32),
            pltpu.VMEM((1, attributes), jnp.int32),
            pltpu.VMEM((2, SIDE, SIDE, DEPTH, *tile), BF16),
            pltpu.VMEM((2, SIDE, SIDE, DEPTH, *tile), BF16),
            pltpu.VMEM((128, SPAN), BF16),
            pltpu.VMEM((count, 128), F32),
            pltpu.VMEM((count, 128), F32),
            pltpu.VMEM((64, count), BF16),
            pltpu.VMEM((SIDE, 64, SPAN), F32),
            *exchange(),
            *exchange(),
            pltpu.VMEM((1, 128), F32),
            pltpu.VMEM((1, 128), F32),
            pltpu.VMEM((SIDE - 1, 1, 128), F32),
            pltpu.VMEM((SIDE * DEPTH, 1, 128), F32),
            pltpu.VMEM((1, 128), F32),
            pltpu.VMEM((1, 128), F32),
            pltpu.VMEM((2, 64, 128), F32),
            pltpu.VMEM((SIDE, 64, 128), F32),
            pltpu.VMEM((SIDE * DEPTH, *row), F32),
            pltpu.VMEM((5, 128), F32),
            pltpu.VMEM((SIDE * DEPTH, 5, 128), F32),
            pltpu.VMEM((1, 128), F32),
            pltpu.VMEM((1, 128), F32),
            pltpu.VMEM((1, 128), F32),
            pltpu.VMEM((SIDE, 1, 128), F32),
            pltpu.SemaphoreType.DMA((6,)),
            pltpu.SemaphoreType.DMA((2, 12)),
            pltpu.SemaphoreType.DMA((2, 3)),
            pltpu.SemaphoreType.DMA((2, 9)),
            pltpu.SemaphoreType.DMA((2, 3)),
            pltpu.SemaphoreType.DMA((3,)),
            pltpu.SemaphoreType.DMA((3,)),
            pltpu.SemaphoreType.DMA((3,)),
            pltpu.SemaphoreType.DMA((3,)),
        ],
        compiler_params=pltpu.CompilerParams(
            collective_id=0, has_side_effects=True, vmem_limit_bytes=63 * 2**20
        ),
        name="pooling_step",
    )(
        doc_length,
        tokens,
        queries,
        norm_gain.reshape(1, -1),
        head_weight,
        head_bias.reshape(1, -1),
        labels.reshape(1, -1),
    )
    sizes = ((rows, attributes), (rows, features), (rows, features), (1, 1), head_weight.shape, (1, attributes))
    outputs = (sizes[4], sizes[5], sizes[2], sizes[3])
    head_grad, bias_grad, query_grad, loss = pl.pallas_call(
        deliver,
        out_shape=tuple(jax.ShapeDtypeStruct(size, F32) for size in outputs),
        in_specs=[hbm] * 4,
        out_specs=(hbm,) * 4,
        scratch_shapes=[pltpu.VMEM(size, F32) for size in sizes] + [pltpu.SemaphoreType.DMA((8,))],
        compiler_params=pltpu.CompilerParams(vmem_limit_bytes=63 * 2**20),
        name="deliver",
    )(wide, normed, query_grad, loss)
    return loss[0, 0], query_grad, head_grad, bias_grad.reshape(-1)


def solution(mesh):
    return jax.shard_map(
        shards,
        mesh=mesh,
        in_specs=(
            P(("ctx", "cls"), None),
            P(),
            P("cls", "ctx"),
            P("ctx"),
            P("ctx", "cls"),
            P("cls"),
            P("cls"),
        ),
        out_specs=(P(), P("cls", "ctx"), P("ctx", "cls"), P("cls")),
        check_vma=False,
    )
```

time: 89.6 us -> 85.8 us (0.958)
  local copies, waits for them, and re-layouts: 6.15 us -> 0 us
  Pallas kernels: 81.8 us -> 84.2 us
    unnamed x13 -> x0, local copies, waits for them, and re-layouts: 5.64 us -> none
    pallas_call x1 -> x2, Pallas kernels: 81.8 us -> 84.2 us  [the longest x1 81.7 us: shards(): pl.pallas_call(kernel, out_shape=(jax.ShapeDtypeStruct((1, 1), F32), jax....]
where the time goes in v2:
time: 85.8 us; the launch traced here: 85.6 us
  Pallas kernels  84.2 us (98%)
  between operations  1.45 us (2%)
    pallas_call x1, Pallas kernels, shards(): pl.pallas_call(kernel, out_shape=(jax.ShapeDtypeStruct((1, 1), F32), jax....  81.7 us
    pallas_call x1, Pallas kernels, shards(): pl.pallas_call(deliver, out_shape=tuple((jax.ShapeDtypeStruct(size, F32)...  2.48 us

profile of v2, /device:TPU:1, one launch (start us, length us, event | category | flops | bytes accessed | tf_op | source)
XLA Modules:
  0.0 85.6 jit_solution(525906263252063793)
XLA Ops:
  1.3 81.7 %pooling_step.1 = (f32[1,1]{1,0:T(1,128)}, f32[8,256]{1,0:T(8,128)}, f32[8,256]{1,0:T(8,128)}, f32[8,512]{1,0:T(8,128)}) custom-call(s32[1]{0:T(128)S(6)} %copy.11.doc_ref, bf16[768,8192]{1,0:T(8,128)(2,1)} %tokens_hbm.1, bf16[8,256]{1,0:T(8,128)(2,1)} %query_hbm.1, f32[1,256]{1,0:T(1,128)} %bitcast.7, bf16[256,512]{1,0:T(8,128)(2,1)} %head_hbm.1, ...), custom_call_target="tpu_custom_call" | custom-call | tf_op jit(solution)/shard_map/pooling_step/pallas_call | solution.py:457
  83.0 2.5 %deliver.1 = (f32[256,512]{1,0:T(8,128)}, f32[1,512]{1,0:T(1,128)}, f32[8,256]{1,0:T(8,128)}, f32[1,1]{1,0:T(1,128)}) custom-call(f32[8,512]{1,0:T(8,128)} %get-tuple-element.12.wide_in, f32[8,256]{1,0:T(8,128)} %get-tuple-element.13.normed_in, f32[8,256]{1,0:T(8,128)} %get-tuple-element.14.query_in, f32[1,1]{1,0:T(1,128)} %get-tuple-element.15.loss_in), custom_call_target="tpu_custom_call" | custom-call | tf_op jit(solution)/shard_map/deliver/pallas_call | solution.py:531

commit v3 on v2

--- a/solution.py
+++ b/solution.py
@@ -21,9 +21,9 @@
 
 
 def kernel(
-    doc_ref, tokens_hbm, query_hbm, gain_hbm, head_hbm, bias_hbm, label_hbm,
+    doc_hbm, tokens_hbm, query_hbm, gain_hbm, head_hbm, bias_hbm, label_hbm,
     loss_ref, query_grad_ref, normed_ref, wide_ref,
-    tok, head, query_ref, gain_ref, bias_ref, label_ref, gathered1, gathered2, rhs, scores, weights, lhs, total,
+    tok, head, doc_ref, query_ref, gain_ref, bias_ref, label_ref, gathered1, gathered2, rhs, scores, weights, lhs, total,
     pair_send1, pair_recv1, a_send1, a_recv1, b_send1, b_recv1,
     pair_send2, pair_recv2, a_send2, a_recv2, b_send2, b_recv2,
     peak_own, peak_pair, peak_a, peak_b, peak_send2, peak_send3, f_pair, f_a, f_b,
@@ -71,7 +71,7 @@
     load_rest = [
         pltpu.make_async_copy(src, dst, load_sem.at[2 + k])
         for k, (src, dst) in enumerate(
-            ((head_hbm, head), (gain_hbm, gain_ref), (bias_hbm, bias_ref), (label_hbm, label_ref))
+            ((head_hbm, head), (gain_hbm, gain_ref), (bias_hbm, bias_ref), (label_hbm, label_ref), (doc_hbm, doc_ref))
         )
     ]
     load_query.start()
@@ -85,9 +85,9 @@
         pl.semaphore_signal(barrier, inc=1, device_id=to, device_id_type=MESH)
 
     for d, dz in plane:
-        greet(on_b(d, dz))
+        greet(at(dx=d, dz=dz))
     for d in range(1, SIDE):
-        greet(on_a(d))
+        greet(at(dy=d))
     greet(partner)
 
     pl.semaphore_wait(barrier, 35)
@@ -96,44 +96,27 @@
         return jnp.concatenate([rows[:, :128], rows[:, 128:]], axis=0)
 
     def gather_begin(g, p, rows):
-        g[c, a, b, z] = split(rows).astype(BF16)
-        own = g.at[c, a, b, z]
+        g[c, y, x, z] = split(rows).astype(BF16)
+        own = g.at[c, y, x, z]
         for d, dz in sorted(plane, key=lambda step: (READY.index(step[0]), -hops(*step))):
-            send(own, own, gather_send.at[p, 0], gather_sems.at[p, d], on_b(d, dz))
+            send(own, own, gather_send.at[p, 0], gather_sems.at[p, d], at(dx=d, dz=dz))
 
     def gather_spread(g, p):
         for d in READY:
-            unit = g.at[c, a, (b + SIDE - d) & 3]
+            unit = g.at[c, y, (x + SIDE - d) & 3]
             take(gather_sems.at[p, d], unit.at[pl.ds(0, 7)] if d == 0 else unit)
-
-            @pl.when(c == 0)
-            def _():
-                for e in (2, 1, 3):
-                    send(unit, unit, gather_send.at[p, 2], gather_sems.at[p, 4 + d], on_a(e))
-
-            @pl.when(c == 1)
-            def _():
-                for e in (1, 3, 2):
-                    send(unit, unit, gather_send.at[p, 2], gather_sems.at[p, 4 + e], on_a(e))
+            for e in (2, 1, 3):
+                send(unit, unit, gather_send.at[p, 2], gather_sems.at[p, 4 + d], at(dy=e))
 
     def gather_sent(g, p):
         take(gather_send.at[p, 0], b_recv1.at[pl.ds(0, 31)])
         take(gather_send.at[p, 1], g.at[0])
         take(gather_send.at[p, 2], g.at[0, pl.ds(0, 3)])
 
-    def gather_forward(g, p, core, j):
-        at_x = (x + SIDE - j) & 3
-
-        @pl.when(c == core)
-        def _():
-            if core == 0:
-                take(gather_sems.at[p, 4 + j], g.at[0, 0, pl.ds(0, 3)])
-                part = g.at[0, :, at_x]
-            else:
-                if j:
-                    take(gather_sems.at[p, 4 + j], g.at[0, 0])
-                part = g.at[1, at_x]
-            send(part, part, gather_send.at[p, 1], gather_sems.at[p, 8 + j], partner)
+    def gather_forward(g, p, j):
+        take(gather_sems.at[p, 4 + j], g.at[0, 0, pl.ds(0, 3)])
+        part = g.at[c, :, (x + SIDE - j) & 3]
+        send(part, part, gather_send.at[p, 1], gather_sems.at[p, 8 + j], partner)
 
     def project(g, p, j, first):
         at_x = ((x + SIDE - j) & 3)
@@ -141,7 +124,7 @@
         for zz in range(DEPTH):
             for yy in range(SIDE):
                 even = g[0, yy, at_x, zz].astype(F32)
-                odd = g[1, at_x, yy, zz].astype(F32)
+                odd = g[1, yy, at_x, zz].astype(F32)
                 for half in range(2):
                     rows = slice(8 * half, 8 * half + 8)
                     col = 256 * zz + 128 * half
@@ -157,16 +140,11 @@
 
     def gather_project(g, p):
         gather_spread(g, p)
-        gather_forward(g, p, 0, READY[0])
-        gather_forward(g, p, 1, READY[0])
+        gather_forward(g, p, READY[0])
         for n, j in enumerate(READY):
             if n < 3:
-                gather_forward(g, p, 0, READY[n + 1])
-            if n in (1, 2):
-                gather_forward(g, p, 1, READY[n + 1])
+                gather_forward(g, p, READY[n + 1])
             project(g, p, j, n == 0)
-            if n == 0:
-                gather_forward(g, p, 1, READY[1])
 
     def pair_begin(p, j, pair_send, pair_recv):
         cols = pl.ds(pl.multiple_of(((x + j) & 3) * SPAN, SPAN), SPAN)
@@ -260,25 +238,26 @@
     rhs[64:, :] = jnp.zeros((64, SPAN), BF16)
     load_query.wait()
     gather_begin(gathered1, 0, query_ref[...].astype(F32))
-    load_tok.wait()
+    for load in [load_tok] + load_rest:
+        load.wait()
     gather_project(gathered1, 0)
 
     @pl.when(c == 1)
     def _():
         for d, dz in plane:
             if d and dz:
-                greet(at(dx=d, dz=dz))
+                greet(at(dy=d, dz=dz))
 
     count = tok.shape[0]
     place = (ctx * 8 + cls) * count + lax.broadcasted_iota(jnp.int32, (count, 128), 0)
-    valid = place < doc_ref[0]
+    valid = place < doc_ref[...]
     masked = jnp.where(valid, scores[...], FAR)
     peak = jnp.max(masked, axis=0, keepdims=True)
     peak_own[...] = peak
     send(peak_own, peak_pair, peak_send.at[0], peak_sems.at[0], partner)
     soft = jnp.where(valid, jnp.exp(masked - peak), 0.0)
     weights[...] = soft
-    lhs[...] = soft.T[:64].astype(BF16)
+    lhs[...] = soft.astype(BF16).T[:64]
 
     first = (0, pair_send1, pair_recv1)
     pair_begin(0, ORDER[0], pair_send1, pair_recv1)
@@ -298,6 +277,10 @@
     for k in range(3):
         peak3 = jnp.maximum(peak3, peak_a[k])
     peak_send3[...] = peak3
+    @pl.when(c == 1)
+    def _():
+        pl.semaphore_wait(barrier, 21)
+
     for d, dz in plane:
         send(peak_send3, peak_b.at[d * DEPTH + dz], peak_send.at[2], peak_sems.at[2], on_b(d, dz))
     f_a[0] = as_column(jnp.exp(peak_send2[...] - peak3))
@@ -318,8 +301,6 @@
         f_b[k] = jnp.broadcast_to(factor, (8, 128))
     pooled = b_end(0, b_send1, b_recv1, True)
 
-    for load in load_rest:
-        load.wait()
     gain = gain_ref[...]
     lane512 = lax.broadcasted_iota(jnp.int32, (8, 512), 1)
     row512 = lax.broadcasted_iota(jnp.int32, (8, 512), 0)
@@ -333,11 +314,6 @@
     square = jnp.sum(pooled * pooled, axis=1, keepdims=True)
     square = jnp.sum(jnp.where(diagonal, square, 0.0), axis=0, keepdims=True)
     part_send[...] = jnp.concatenate([product[:, 128 * k : 128 * k + 128] for k in range(4)] + [square], axis=0)
-
-    @pl.when(c == 1)
-    def _():
-        pl.semaphore_wait(barrier, 21)
-
     for d, dz in plane:
         send(part_send, part_recv.at[ctx], misc_send.at[0], misc_sems.at[0], at(dx=d, dz=dz))
     part_recv[ctx] = part_send[...]
@@ -379,7 +355,7 @@
     for d in range(1, SIDE):
         send(loss_send2, loss_y.at[y], misc_send.at[2], misc_sems.at[2], at(dy=d))
     loss_y[y] = loss_send2[...]
-    lhs[...] = (weights[...] * scores[...]).T[:64].astype(BF16)
+    lhs[...] = (weights[...] * scores[...]).astype(BF16).T[:64]
 
     pair_begin(1, ORDER[0], pair_send2, pair_recv2)
     for n in range(1, SIDE):
@@ -463,7 +439,7 @@
             jax.ShapeDtypeStruct((rows, attributes), F32),
         ),
         in_specs=[
-            pl.BlockSpec(memory_space=pltpu.SMEM),
+            hbm,
             hbm,
             hbm,
             hbm,
@@ -475,6 +451,7 @@
         scratch_shapes=[
             pltpu.VMEM((count, width), BF16),
             pltpu.VMEM(head_weight.shape, BF16),
+            pltpu.VMEM((1, 1), jnp.int32),
             pltpu.VMEM(queries.shape, BF16),
             pltpu.VMEM((1, features), F32),
             pltpu.VMEM((1, attributes), F32),
@@ -503,7 +480,7 @@
             pltpu.VMEM((1, 128), F32),
             pltpu.VMEM((1, 128), F32),
             pltpu.VMEM((SIDE, 1, 128), F32),
-            pltpu.SemaphoreType.DMA((6,)),
+            pltpu.SemaphoreType.DMA((7,)),
             pltpu.SemaphoreType.DMA((2, 12)),
             pltpu.SemaphoreType.DMA((2, 3)),
             pltpu.SemaphoreType.DMA((2, 9)),
@@ -518,7 +495,7 @@
         ),
         name="pooling_step",
     )(
-        doc_length,
+        doc_length.reshape(1, 1),
         tokens,
         queries,
         norm_gain.reshape(1, -1),

time: 85.8 us -> 84.9 us (0.990)
  Pallas kernels: 84.2 us -> 83.3 us
where the time goes in v3:
time: 84.9 us; the launch traced here: 84.8 us
  Pallas kernels  83.3 us (98%)
  between operations  1.45 us (2%)
    pallas_call x1, Pallas kernels, shards(): pl.pallas_call(kernel, out_shape=(jax.ShapeDtypeStruct((1, 1), F32), jax....  80.8 us
    pallas_call x1, Pallas kernels, shards(): pl.pallas_call(deliver, out_shape=tuple((jax.ShapeDtypeStruct(size, F32)...  2.49 us

profile of v3, /device:TPU:1, one launch (start us, length us, event | category | flops | bytes accessed | tf_op | source)
XLA Modules:
  0.0 84.8 jit_solution(13343125944113246285)
XLA Ops:
  1.3 80.8 %pooling_step.1 = (f32[1,1]{1,0:T(1,128)}, f32[8,256]{1,0:T(8,128)}, f32[8,256]{1,0:T(8,128)}, f32[8,512]{1,0:T(8,128)}) custom-call(s32[1,1]{1,0:T(1,128)} %bitcast.6.doc_hbm, bf16[768,8192]{1,0:T(8,128)(2,1)} %tokens_hbm.1, bf16[8,256]{1,0:T(8,128)(2,1)} %query_hbm.1, f32[1,256]{1,0:T(1,128)} %bitcast.9, bf16[256,512]{1,0:T(8,128)(2,1)} %head_hbm.1, ...), custom_call_target="tpu_custom_call" | custom-call | tf_op jit(solution)/shard_map/pooling_step/pallas_call | solution.py:433
  82.1 2.5 %deliver.1 = (f32[256,512]{1,0:T(8,128)}, f32[1,512]{1,0:T(1,128)}, f32[8,256]{1,0:T(8,128)}, f32[1,1]{1,0:T(1,128)}) custom-call(f32[8,512]{1,0:T(8,128)} %get-tuple-element.12.wide_in, f32[8,256]{1,0:T(8,128)} %get-tuple-element.13.normed_in, f32[8,256]{1,0:T(8,128)} %get-tuple-element.14.query_in, f32[1,1]{1,0:T(1,128)} %get-tuple-element.15.loss_in), custom_call_target="tpu_custom_call" | custom-call | tf_op jit(solution)/shard_map/deliver/pallas_call | solution.py:508
